TPU v7x, 32 devices: a whole 2x2x4 slice. The times are simulated.
32 devices in a mesh: dp: 4 (over y, core), tensor: 8 (over z, x).
Axes of the slice: x: 2, y: 2, z: 4, core: 2. Of those that a mesh axis runs over, the one named last changes fastest.
Arguments:
- attn_in: bfloat16 [512, 2048], P('dp', 'tensor'), parts along dimension 0, may hold values from -127 to 127
- wo_int: bfloat16 [2048, 8192], P('tensor'), may hold values from -127 to 127
- wo_exponent: int32 [8192], replicated, may hold values from -15 to -12
- token_scale: float32 [512], P(('dp', 'tensor')), parts along dimension 0, may hold values from 0.3 to 3
- residual: bfloat16 [512, 8192], P(('dp', 'tensor')), parts along dimension 0, may hold values from -6 to 6
- norm_gain: float32 [8192], replicated, may hold values from 0.5 to 1.5
- gate_int: bfloat16 [8192, 2048], P(None, 'tensor'), may hold values from -127 to 127, as said below
- up_int: bfloat16 [8192, 2048], P(None, 'tensor'), may hold values from -127 to 127, as said below
- gate_exponent: int32 [2048], P('tensor'), may hold values from -14 to -12
- up_exponent: int32 [2048], P('tensor'), may hold values from -14 to -12
Outputs:
- hidden: bfloat16 [512, 2048], P('dp', 'tensor'), parts along dimension 0
- checksum: float32 [32, 8192], P(('dp', 'tensor')), parts along dimension 0
There are 4 independent parts, one for each index of `dp`. A program takes and returns all parts, laid end to end along the dimension named above; an argument that names none is the same for every part. Nothing has to cross between parts.
Inputs may be any that keep to these rules, and one draw needn't show every extreme that they name: `gate_int`: integer values. `up_int`: integer values.
All inputs are finite; a program needn't handle non-finite values.
Results may differ from a plain program's by a relative error of at most 0.035.
Values may be sent and summed in bfloat16 or wider, within the bound.
A program may use at most 64 MiB of HBM per device.

v0:
```python
import jax
import jax.numpy as jnp
from jax import lax
from jax.sharding import PartitionSpec as P


def normalize(stream, norm_gain):
    widened = stream.astype(jnp.float32)
    inverse = lax.rsqrt(jnp.mean(widened * widened, axis=1, keepdims=True) + 1e-05)
    return (widened * inverse * norm_gain[None, :]).astype(jnp.bfloat16)


def quantize(normed_low):
    widened = lax.optimization_barrier(normed_low).astype(jnp.float32)
    largest = jnp.max(jnp.abs(widened), axis=1, keepdims=True)
    xscale = ((largest + 1e-06) / 127.0).astype(jnp.bfloat16)
    levels = jnp.floor(widened / xscale.astype(jnp.float32) + 0.5).astype(jnp.bfloat16)
    return (levels, xscale)


def local(
    attn_in,
    wo_int,
    wo_exponent,
    token_scale,
    residual,
    norm_gain,
    gate_int,
    up_int,
    gate_exponent,
    up_exponent,
):
    groups = lax.axis_size("tensor")
    own_rows = residual.shape[0]
    col_scale = jnp.exp2(wo_exponent.astype(jnp.float32))
    gate_scale = jnp.exp2(gate_exponent.astype(jnp.float32))[None, :]
    up_scale = jnp.exp2(up_exponent.astype(jnp.float32))[None, :]
    partial_value = jnp.dot(attn_in, wo_int, preferred_element_type=jnp.float32)
    block_sums = jnp.sum(partial_value.reshape(groups, own_rows, partial_value.shape[1]), axis=1)
    owned_rows, col_total = (
        lax.psum_scatter(partial_value, "tensor", scatter_dimension=0, tiled=True),
        lax.psum_scatter(block_sums, "tensor", scatter_dimension=0, tiled=True),
    )
    checksum = col_total * col_scale[None, :] / own_rows
    attn_out = owned_rows * token_scale[:, None] * col_scale[None, :]
    stream = (residual.astype(jnp.float32) + attn_out).astype(jnp.bfloat16)
    normed_low = normalize(stream, norm_gain)
    all_normed = lax.all_gather(normed_low, "tensor", axis=0, tiled=True)
    levels, xscale = quantize(all_normed)
    row_scale = xscale.astype(jnp.float32)
    gate_sum = (
        jnp.dot(levels, gate_int, preferred_element_type=jnp.float32) * row_scale * gate_scale
    )
    up_sum = jnp.dot(levels, up_int, preferred_element_type=jnp.float32) * row_scale * up_scale
    hidden = (jax.nn.silu(gate_sum) * up_sum).astype(jnp.bfloat16)
    return (hidden, checksum)


def solution(mesh):
    placed = (
        P("dp", "tensor"),
        P("tensor", None),
        P(),
        P(("dp", "tensor")),
        P(("dp", "tensor"), None),
        P(),
        P(None, "tensor"),
        P(None, "tensor"),
        P("tensor"),
        P("tensor"),
    )
    return jax.shard_map(
        local,
        mesh=mesh,
        in_specs=placed,
        out_specs=(P("dp", "tensor"), P(("dp", "tensor"), None)),
        check_vma=False,
    )
```

profile of v0, /device:TPU:0, one launch (start us, length us, event | category | flops | bytes accessed | tf_op | source)
XLA Modules:
  0.0 244.5 jit_solution(15121296481471116367)
XLA Ops:
  7.2 0.0 copy-start
  7.2 0.0 reduce-scatter.2.cloned.1.call-start
  7.2 0.8 copy-done
  8.0 6.1 %bitcast_reduce_fusion = (f32[8,8192]{1,0:T(8,128)}, f32[128,8192]{1,0:T(8,128)}) fusion(bf16[128,256]{1,0:T(8,128)(2,1)S(1)} %copy-done, bf16[256,8192]{1,0:T(8,128)(2,1)} %param.11), kind=kOutput, calls=%fused_computation.6 | convolution fusion | flops 537853952 | bytes 8716288 | tf_op jit(solution)/shard_map/dot_general | solution.py:38
  14.1 0.0 copy-start.4
  14.1 0.0 copy-start.2
  14.1 0.0 copy-start.7
  14.1 0.0 copy-start.3
  14.1 0.0 copy-start.9
  14.1 0.0 copy-start.5
  14.1 0.0 copy-start.6
  14.1 0.0 reduce-scatter.2.cloned.1.call-update
  14.1 0.0 all-reduce.3.cloned.1.call-start
  14.2 0.7 all-reduce.3.cloned.1.call-update
  14.9 0.0 all-gather.2.cloned.1.call-start
  14.9 0.0 copy-done.4
  15.0 90.1 %reduce-scatter.2.cloned.1.call-done = f32[16,8192]{1,0:T(8,128)} async-done(((f32[128,8192]{1,0:T(8,128)}), f32[16,8192]{1,0:T(8,128)}) %reduce-scatter.2.cloned.1.call-update) | async-done | bytes 524304 | tf_op jit(solution)/shard_map/reduce_scatter | solution.py:41
  105.1 0.0 copy-done.2
  105.1 0.0 copy-done.7
  105.1 1.3 fusion.8
  106.4 0.0 copy-done.3
  106.4 0.8 fusion.10
  107.3 0.0 all-gather.2.cloned.1.call-update
  107.3 0.0 copy-done.9
  107.3 0.6 dynamic-slice
  107.9 0.0 copy-done.5
  107.9 0.0 copy-done.6
  107.9 71.2 %all-reduce.3.cloned.1.call-done = f32[8,8192]{1,0:T(8,128)} async-done(((f32[8,8192]{1,0:T(8,128)}), f32[8,8192]{1,0:T(8,128)}) %all-reduce.3.cloned.1.call-update) | async-done | bytes 262160
  179.1 2.3 fusion.11
  181.4 48.5 %all-gather.2.cloned.1.call-done = bf16[128,8192]{1,0:T(8,128)(2,1)} async-done(((bf16[16,8192]{1,0:T(8,128)(2,1)}), bf16[128,8192]{1,0:T(8,128)(2,1)}) %all-gather.2.cloned.1.call-update) | async-done | bytes 2097168 | tf_op jit(solution)/shard_map/all_gather | solution.py:48
  229.8 2.0 fusion
  231.9 0.0 copy-start.1
  231.9 0.0 copy-start.8
  231.9 3.8 %fusion.6 = f32[128,256]{1,0:T(8,128)S(1)} fusion(bf16[8192,256]{1,0:T(8,128)(2,1)} %param.16, f32[256]{0:T(256)S(1)} %multiply_exponential_fusion.2, f32[128]{0:T(128)S(1)} %convert_convert_fusion, bf16[128,8192]{1,0:T(8,128)(2,1)} %all-gather.2.cloned.1.call-done), kind=kOutput, calls=%fused_computation.11 | convolution fusion | flops 542179328 | bytes 6424064 | tf_op jit(solution)/shard_map/dot_general | solution.py:52
  235.7 0.0 copy-done.1
  235.7 0.8 copy-done.8
  236.5 1.5 fusion.7
  (5 shorter events, 0.0 us)
Async XLA Ops:
  7.2 0.8 copy-start
  7.2 97.9 %reduce-scatter.2.cloned.1.call-start = ((), (), s32[]{:S(2)}) async-start(), calls=%async_computation.1 | async-start | bytes 4718592 | tf_op jit(solution)/shard_map/reduce_scatter | solution.py:41
  14.1 0.9 copy-start.4
  14.1 91.0 %copy-start.2 = (bf16[16,8192]{1,0:T(8,128)(2,1)S(1)}, bf16[16,8192]{1,0:T(8,128)(2,1)}, u32[]{:S(2)}) copy-start(bf16[16,8192]{1,0:T(8,128)(2,1)} %param.14) | copy-start | bytes 786436
  14.1 91.0 %copy-start.7 = (f32[16]{0:T(128)S(1)}, f32[16]{0:T(128)}, u32[]{:S(2)}) copy-start(f32[16]{0:T(128)} %param.13) | copy-start | bytes 196
  14.1 92.3 %copy-start.3 = (f32[8192]{0:T(1024)S(1)}, f32[8192]{0:T(1024)}, u32[]{:S(2)}) copy-start(f32[8192]{0:T(1024)} %param.15) | copy-start | bytes 98308
  14.1 93.2 %copy-start.9 = (u32[32]{0:T(128)S(1)}, u32[32]{0:T(128)}, u32[]{:S(2)}) copy-start(u32[32]{0:T(128)} %constant.29) | copy-start | bytes 388
  14.1 93.8 %copy-start.5 = (s32[256]{0:T(256)S(1)}, s32[256]{0:T(256)}, u32[]{:S(2)}) copy-start(s32[256]{0:T(256)} %param.18) | copy-start | bytes 3076
  14.1 93.8 %copy-start.6 = (s32[256]{0:T(256)S(1)}, s32[256]{0:T(256)}, u32[]{:S(2)}) copy-start(s32[256]{0:T(256)} %param.19) | copy-start | bytes 3076
  14.1 165.0 %all-reduce.3.cloned.1.call-start = ((), (), s32[]{:S(2)}) async-start(), calls=%async_computation.3 | async-start | bytes 524288
  14.9 214.9 %all-gather.2.cloned.1.call-start = ((), (), s32[]{:S(2)}) async-start(), calls=%async_computation.2 | async-start | bytes 2359296 | tf_op jit(solution)/shard_map/all_gather | solution.py:48
  231.9 3.8 %copy-start.1 = (bf16[128,8192]{1,0:T(8,128)(2,1)S(1)}, bf16[128,8192]{1,0:T(8,128)(2,1)}, u32[]{:S(2)}) copy-start(bf16[128,8192]{1,0:T(8,128)(2,1)} %all-gather.2.cloned.1.call-done) | copy-start | bytes 6291460
  231.9 4.7 %copy-start.8 = (bf16[8192,256]{1,0:T(8,128)(2,1)S(1)}, bf16[8192,256]{1,0:T(8,128)(2,1)}, u32[]{:S(2)}) copy-start(bf16[8192,256]{1,0:T(8,128)(2,1)} %param.17) | copy-start | bytes 12582916
Sparse Core Ops, SparseCore 0:
  14.3 90.7 reduce-scatter.1
  108.8 70.2 all-reduce.2
  181.2 48.5 all-gather.1
where the time goes:
time: 245 us
  waiting for transfers between devices  210 us (86%)
  between operations  13.9 us (6%)
  matrix products  11.3 us (5%)
  other arithmetic  6.49 us (3%)
    reduce_scatter x1, waiting for transfers between devices, local(): lax.psum_scatter(partial_value, 'tensor', scatter_dimension=0, tiled=True)  90.1 us
    unnamed x4, waiting for transfers between devices  71.9 us
    all_gather x1, waiting for transfers between devices, local(): all_normed = lax.all_gather(normed_low, 'tensor', axis=0, tiled=True)  48.5 us
    dot_general x1, matrix products, local(): partial_value = jnp.dot(attn_in, wo_int, preferred_element_type=jnp.float32)  6.06 us
  transfers between devices with their start and end apart: 3, of which 3 were waited for; matrix products, arithmetic and copies ran while one was open for 2% of the time, Pallas kernels for 0%

commit v1 on v0

v1 whole, which is shorter than its diff:
```python
import functools

import jax
import jax.numpy as jnp
from jax import lax
from jax.experimental import pallas as pl
from jax.experimental.pallas import tpu as pltpu
from jax.sharding import PartitionSpec as P

MESH = pl.DeviceIdType.MESH
ROWS = 16
EXTRA = 128


def pack(value, dst):
    width = value.shape[1]
    largest = jnp.max(jnp.abs(value), axis=1, keepdims=True)
    exponent = jnp.ceil(jnp.log2(jnp.maximum(largest, 1e-30) * (1.0 / 32000.0)))
    steps = jnp.floor(value * jnp.exp2(-exponent) + 0.5)
    dst[:, :width] = steps.astype(jnp.int32).astype(jnp.int16)
    dst[:, width:] = jnp.broadcast_to(exponent, (value.shape[0], EXTRA)).astype(jnp.int32).astype(jnp.int16)


def unpack(src):
    width = src.shape[1] - EXTRA
    exponent = src[:, width:].astype(jnp.int32).astype(jnp.float32)[:, :1]
    return src[:, :width].astype(jnp.int32).astype(jnp.float32) * jnp.exp2(exponent)


def kernel(
    X, Z, nch,
    attn, wo, wo_exp, token_scale, residual, gain, gate, up, gate_exp, up_exp,
    hidden, checksum,
    wo_v, gate_v, up_v, a_rel, part, keep, xs, xr, zs, zr, total, lev, gate_acc, up_acc,
    wo_sem, weight_sem, xs_sem, xr_sem, zs_sem, zr_sem, gzs_sem, gzr_sem, gxs_sem, gxr_sem,
):
    D = wo.shape[1]
    cw = D // nch
    me = lax.axis_index("tensor")
    z, x = me // X, lax.rem(me, X)
    zrows = Z * ROWS

    def x_peer(d):
        return {"tensor": z * X + lax.rem(x + d, X)}

    def z_peer(d):
        return {"tensor": lax.rem(z + d, Z) * X + x}

    def block_of(d, dz):
        return lax.rem(z + dz, Z) * X + lax.rem(x + d, X)

    def cols(c):
        return pl.ds(pl.multiple_of(c * cw, cw), cw)

    def wo_copy(c):
        return pltpu.make_async_copy(wo.at[:, cols(c)], wo_v.at[:, cols(c)], wo_sem.at[c])

    def remote(src, dst, send, recv, peer):
        return pltpu.make_async_remote_copy(
            src_ref=src, dst_ref=dst, send_sem=send, recv_sem=recv, device_id=peer, device_id_type=MESH
        )

    def x_copy(d, c):
        return remote(xs.at[d - 1, c], xr.at[d - 1, c], xs_sem.at[d - 1, c], xr_sem.at[d - 1, c], x_peer(d))

    def z_copy(d, c):
        return remote(zs.at[d - 1, c], zr.at[d - 1, c], zs_sem.at[d - 1, c], zr_sem.at[d - 1, c], z_peer(d))

    def gz_copy(d, c):
        return remote(
            lev.at[c, pl.ds(0, ROWS)], lev.at[c, pl.ds((Z - d) * ROWS, ROWS)],
            gzs_sem.at[d - 1, c], gzr_sem.at[d - 1, c], z_peer(d),
        )

    def gx_copy(d, c):
        return remote(
            lev.at[c, pl.ds(0, zrows)], lev.at[c, pl.ds((X - d) * zrows, zrows)],
            gxs_sem.at[d - 1, c], gxr_sem.at[d - 1, c], x_peer(d),
        )

    def loop(body):
        lax.fori_loop(0, nch, lambda c, _: (body(c), 0)[1], 0)

    loop(lambda c: wo_copy(c).start())
    gate_copy = pltpu.make_async_copy(gate, gate_v, weight_sem.at[0])
    up_copy = pltpu.make_async_copy(up, up_v, weight_sem.at[1])
    gate_copy.start()
    up_copy.start()

    barrier = pltpu.get_barrier_semaphore()
    for d in range(1, X):
        pl.semaphore_signal(barrier, inc=1, device_id=x_peer(d), device_id_type=MESH)
    for d in range(1, Z):
        pl.semaphore_signal(barrier, inc=1, device_id=z_peer(d), device_id_type=MESH)

    for d in range(X):
        for dz in range(Z):
            a_rel[pl.ds((d * Z + dz) * ROWS, ROWS), :] = attn[
                pl.ds(pl.multiple_of(block_of(d, dz) * ROWS, ROWS), ROWS), :
            ]
    pl.semaphore_wait(barrier, X + Z - 2)

    def project(c):
        wo_copy(c).wait()
        part[...] = jnp.dot(a_rel[...], wo_v[:, cols(c)], preferred_element_type=jnp.float32)
        for d in range(1, X):
            for dz in range(Z):
                pack(part[pl.ds((d * Z + dz) * ROWS, ROWS), :], xs.at[d - 1, c, pl.ds(dz * ROWS, ROWS)])
            x_copy(d, c).start()
        keep[c] = part[:zrows, :]

    loop(project)

    def add_x(c):
        for d in range(1, X):
            x_copy(d, c).wait_recv()
        for step in range(1, Z + 1):
            dz = step % Z
            rows = pl.ds(dz * ROWS, ROWS)
            value = keep[c, rows, :]
            for d in range(1, X):
                value = value + unpack(xr.at[d - 1, c, rows])
            if dz:
                pack(value, zs.at[dz - 1, c])
                z_copy(dz, c).start()
            else:
                total[c] = value

    loop(add_x)

    row_of = lax.broadcasted_iota(jnp.int32, (ROWS, 1), 0)
    row_scale = jnp.zeros((ROWS, 1), jnp.float32)
    for i in range(ROWS):
        row_scale = jnp.where(row_of == i, token_scale[i], row_scale)

    def add_z(c, squares):
        for d in range(1, Z):
            z_copy(d, c).wait_recv()
        value = total[c]
        for d in range(1, Z):
            value = value + unpack(zr.at[d - 1, c])
        col_scale = jnp.exp2(wo_exp[:, cols(c)].astype(jnp.float32))
        checksum[:, cols(c)] = jnp.sum(value, axis=0, keepdims=True) * col_scale / ROWS
        stream = residual[:, cols(c)].astype(jnp.float32) + value * row_scale * col_scale
        stream = stream.astype(jnp.bfloat16).astype(jnp.float32)
        total[c] = stream
        return squares + jnp.sum(stream * stream, axis=1, keepdims=True)

    squares = lax.fori_loop(0, nch, add_z, jnp.zeros((ROWS, 1), jnp.float32))
    inverse = lax.rsqrt(squares / D + 1e-05)

    def norm(c, largest):
        low = (total[c] * inverse * gain[:, cols(c)]).astype(jnp.bfloat16).astype(jnp.float32)
        total[c] = low
        return jnp.maximum(largest, jnp.max(jnp.abs(low), axis=1, keepdims=True))

    largest = lax.fori_loop(0, nch, norm, jnp.zeros((ROWS, 1), jnp.float32))
    xscale = ((largest + 1e-06) / 127.0).astype(jnp.bfloat16)
    xwide = xscale.astype(jnp.float32)

    def send(c):
        lev[c, :ROWS, :cw] = jnp.floor(total[c] / xwide + 0.5).astype(jnp.bfloat16)
        lev[c, :ROWS, cw:] = jnp.broadcast_to(xwide, (ROWS, EXTRA)).astype(jnp.bfloat16)
        for d in range(1, Z):
            gz_copy(d, c).start()

    loop(send)
    gate_acc[...] = jnp.zeros_like(gate_acc)
    up_acc[...] = jnp.zeros_like(up_acc)
    gate_copy.wait()
    up_copy.wait()

    def forward(c):
        for d in range(1, Z):
            gz_copy(d, c).wait_recv()
        for d in range(1, X):
            gx_copy(d, c).start()

    def multiply(c):
        for d in range(1, X):
            gx_copy(d, c).wait_recv()
        levels = lev[c, :, :cw]
        gate_acc[...] += jnp.dot(levels, gate_v[cols(c), :], preferred_element_type=jnp.float32)
        up_acc[...] += jnp.dot(levels, up_v[cols(c), :], preferred_element_type=jnp.float32)

    forward(0)

    def gather(c, _):
        forward(c + 1)
        multiply(c)
        return 0

    lax.fori_loop(0, nch - 1, gather, 0)
    multiply(nch - 1)

    gate_scale = jnp.exp2(gate_exp[...].astype(jnp.float32))
    up_scale = jnp.exp2(up_exp[...].astype(jnp.float32))
    for d in range(X):
        for dz in range(Z):
            rows = pl.ds((d * Z + dz) * ROWS, ROWS)
            scale = lev[0, rows, cw:].astype(jnp.float32)[:, :1]
            g = gate_acc[rows, :] * scale * gate_scale
            u = up_acc[rows, :] * scale * up_scale
            value = g / (1.0 + jnp.exp(-g)) * u
            hidden[pl.ds(pl.multiple_of(block_of(d, dz) * ROWS, ROWS), ROWS), :] = value.astype(jnp.bfloat16)

    def drain(c):
        for d in range(1, X):
            x_copy(d, c).wait_send()
            gx_copy(d, c).wait_send()
        for d in range(1, Z):
            z_copy(d, c).wait_send()
            gz_copy(d, c).wait_send()

    loop(drain)


def local(n, attn_in, wo_int, wo_exponent, token_scale, residual, norm_gain, gate_int, up_int, gate_exponent, up_exponent):
    Z = 4 if n % 4 == 0 else 1
    X = n // Z
    D = wo_int.shape[1]
    nch = 8
    cw = D // nch
    rows, ff = attn_in.shape[0], gate_int.shape[1]
    vmem = pl.BlockSpec(memory_space=pltpu.VMEM)
    anywhere = pl.BlockSpec(memory_space=pl.ANY)
    dma = pltpu.SemaphoreType.DMA
    xn, zn = max(X - 1, 1), max(Z - 1, 1)
    return pl.pallas_call(
        functools.partial(kernel, X, Z, nch),
        out_shape=(
            jax.ShapeDtypeStruct((rows, ff), jnp.bfloat16),
            jax.ShapeDtypeStruct((1, D), jnp.float32),
        ),
        in_specs=[
            vmem, anywhere, vmem, pl.BlockSpec(memory_space=pltpu.SMEM), vmem, vmem, anywhere, anywhere, vmem, vmem,
        ],
        out_specs=(vmem, vmem),
        scratch_shapes=[
            pltpu.VMEM(wo_int.shape, jnp.bfloat16),
            pltpu.VMEM(gate_int.shape, jnp.bfloat16),
            pltpu.VMEM(up_int.shape, jnp.bfloat16),
            pltpu.VMEM(attn_in.shape, jnp.bfloat16),
            pltpu.VMEM((rows, cw), jnp.float32),
            pltpu.VMEM((nch, Z * ROWS, cw), jnp.float32),
            pltpu.VMEM((xn, nch, Z * ROWS, cw + EXTRA), jnp.int16),
            pltpu.VMEM((xn, nch, Z * ROWS, cw + EXTRA), jnp.int16),
            pltpu.VMEM((zn, nch, ROWS, cw + EXTRA), jnp.int16),
            pltpu.VMEM((zn, nch, ROWS, cw + EXTRA), jnp.int16),
            pltpu.VMEM((nch, ROWS, cw), jnp.float32),
            pltpu.VMEM((nch, rows, cw + EXTRA), jnp.bfloat16),
            pltpu.VMEM((rows, ff), jnp.float32),
            pltpu.VMEM((rows, ff), jnp.float32),
            dma((nch,)),
            dma((2,)),
            dma((xn, nch)),
            dma((xn, nch)),
            dma((zn, nch)),
            dma((zn, nch)),
            dma((zn, nch)),
            dma((zn, nch)),
            dma((xn, nch)),
            dma((xn, nch)),
        ],
        compiler_params=pltpu.CompilerParams(
            collective_id=0, has_side_effects=True, vmem_limit_bytes=48 * 1024 * 1024
        ),
        cost_estimate=pl.CostEstimate(
            flops=2 * rows * D * (attn_in.shape[1] + 2 * ff), bytes_accessed=2 * D * (attn_in.shape[1] + 2 * ff),
            transcendentals=rows * ff,
        ),
    )(
        attn_in, wo_int, wo_exponent.reshape(1, D), token_scale, residual, norm_gain.reshape(1, D),
        gate_int, up_int, gate_exponent.reshape(1, ff), up_exponent.reshape(1, ff),
    )


def solution(mesh):
    placed = (
        P("dp", "tensor"),
        P("tensor", None),
        P(),
        P(("dp", "tensor")),
        P(("dp", "tensor"), None),
        P(),
        P(None, "tensor"),
        P(None, "tensor"),
        P("tensor"),
        P("tensor"),
    )
    return jax.shard_map(
        functools.partial(local, mesh.shape["tensor"]),
        mesh=mesh,
        in_specs=placed,
        out_specs=(P("dp", "tensor"), P(("dp", "tensor"), None)),
        check_vma=False,
    )
```

time: 245 us -> 85.2 us (0.35)
  waiting for transfers between devices: 210 us -> 0 us
  Pallas kernels: 0 us -> 75.4 us
  between operations: 13.9 us -> 0.66 us
  matrix products: 11.3 us -> 0 us
  other arithmetic: 6.49 us -> 0 us
  local copies, waits for them, and re-layouts: 2.26 us -> 8.74 us
    reduce_scatter x1 -> x0, waiting for transfers between devices: 90.1 us -> none  [local(): lax.psum_scatter(partial_value, 'tensor', scatter_dimension=0, tiled=True)]
    pallas_call x0 -> x1, Pallas kernels: none -> 75.4 us  [local(): pl.pallas_call(functools.partial(kernel, X, Z, nch), out_shape=(jax.Shape...]
    unnamed x4 -> x0, waiting for transfers between devices: 71.9 us -> none
    all_gather x1 -> x0, waiting for transfers between devices: 48.5 us -> none  [local(): all_normed = lax.all_gather(normed_low, 'tensor', axis=0, tiled=True)]
    dot_general x3 -> x0, matrix products: 11.3 us -> none  [the longest x1 6.06 us: local(): partial_value = jnp.dot(attn_in, wo_int, preferred_element_type=jnp.float32)]
    unnamed x21 -> x18, local copies, waits for them, and re-layouts: 2.26 us -> 8.74 us
  transfers between devices with their start and end apart: 3 -> 0, of which waited for: 3 -> 0; matrix products, arithmetic and copies ran while one was open for 2% -> 0% of each run, Pallas kernels for 0% -> 0%
where the time goes in v1:
time: 85.2 us; the launch traced here: 84.8 us
  Pallas kernels  75.4 us (88%)
  local copies, waits for them, and re-layouts  8.74 us (10%)
    pallas_call x1, Pallas kernels, local(): pl.pallas_call(functools.partial(kernel, X, Z, nch), out_shape=(jax.Shape...  75.4 us
    unnamed x18, local copies, waits for them, and re-layouts  8.74 us

profile of v1, /device:TPU:0, one launch (start us, length us, event | category | flops | bytes accessed | tf_op | source)
XLA Modules:
  0.0 84.8 jit_solution(9101713756819651563)
XLA Ops:
  0.6 0.0 copy-start
  0.6 2.2 %copy-done = bf16[256,8192]{1,0:T(8,128)(2,1)S(1)} copy-done((bf16[256,8192]{1,0:T(8,128)(2,1)S(1)}, bf16[256,8192]{1,0:T(8,128)(2,1)}, u32[]{:S(2)}) %copy-start) | copy-done | bytes 4194328
  2.8 0.0 copy-start.1
  2.8 0.9 %copy-done.1 = bf16[16,8192]{1,0:T(8,128)(2,1)S(1)} copy-done((bf16[16,8192]{1,0:T(8,128)(2,1)S(1)}, bf16[16,8192]{1,0:T(8,128)(2,1)}, u32[]{:S(2)}) %copy-start.1) | copy-done | bytes 262168
  3.8 0.0 copy-start.2
  3.8 0.8 copy-done.2
  4.6 0.0 copy-start.3
  4.6 0.8 copy-done.3
  5.4 0.0 copy-start.4
  5.4 0.8 copy-done.4
  6.1 0.0 copy-start.5
  6.1 0.7 copy-done.5
  6.8 0.0 copy-start.6
  6.8 0.7 copy-done.6
  7.5 0.0 copy-start.7
  7.5 0.7 copy-done.7
  8.1 75.4 %shard_map.113 = (bf16[128,256]{1,0:T(8,128)(2,1)S(1)}, f32[1,8192]{1,0:T(1,128)S(1)}) custom-call(bf16[128,256]{1,0:T(8,128)(2,1)S(1)} %copy-done.2, bf16[256,8192]{1,0:T(8,128)(2,1)S(1)} %copy-done, s32[1,8192]{1,0:T(1,128)S(1)} %bitcast.4, f32[16]{0:T(128)S(1)} %copy-done.7, bf16[16,8192]{1,0:T(8,128)(2,1)S(1)} %copy-done.1, f32[1,8192]{1,0:T(1,128)S(1)} %bitcast.5, ...), custom_call_target="tpu_custom_call" | custom-call | flops 1610612736 | bytes 12582912 | tf_op jit(solution)/shard_map/pallas_call | solution.py:229
  83.5 0.6 copy.14
  84.2 0.6 copy.15
Async XLA Ops:
  0.6 2.2 %copy-start = (bf16[256,8192]{1,0:T(8,128)(2,1)S(1)}, bf16[256,8192]{1,0:T(8,128)(2,1)}, u32[]{:S(2)}) copy-start(bf16[256,8192]{1,0:T(8,128)(2,1)} %wo.1) | copy-start | bytes 12582916
  2.8 0.9 %copy-start.1 = (bf16[16,8192]{1,0:T(8,128)(2,1)S(1)}, bf16[16,8192]{1,0:T(8,128)(2,1)}, u32[]{:S(2)}) copy-start(bf16[16,8192]{1,0:T(8,128)(2,1)} %residual.1) | copy-start | bytes 786436
  3.8 0.8 copy-start.2
  4.6 0.8 copy-start.3
  5.4 0.8 copy-start.4
  6.1 0.7 copy-start.5
  6.8 0.7 copy-start.6
  7.5 0.7 copy-start.7

commit v2 on v1

--- a/solution.py
+++ b/solution.py
@@ -29,10 +29,11 @@
 
 def kernel(
     X, Z, nch,
-    attn, wo, wo_exp, token_scale, residual, gain, gate, up, gate_exp, up_exp,
+    attn_h, wo, wo_exp_h, token_scale_h, residual_h, gain_h, gate, up, gate_exp_h, up_exp_h,
     hidden, checksum,
-    wo_v, gate_v, up_v, a_rel, part, keep, xs, xr, zs, zr, total, lev, gate_acc, up_acc,
-    wo_sem, weight_sem, xs_sem, xr_sem, zs_sem, zr_sem, gzs_sem, gzr_sem, gxs_sem, gxr_sem,
+    attn, wo_exp, token_scale, residual, gain, gate_exp, up_exp,
+    wo_v, gate_v, up_v, a_rel, part, keep, xs, xr, zs, zr, total, lev, scales, gate_acc, up_acc,
+    small_sem, wo_sem, weight_sem, xs_sem, xr_sem, zs_sem, zr_sem, gs_sem, gr_sem,
 ):
     D = wo.shape[1]
     cw = D // nch
@@ -66,22 +67,56 @@
     def z_copy(d, c):
         return remote(zs.at[d - 1, c], zr.at[d - 1, c], zs_sem.at[d - 1, c], zr_sem.at[d - 1, c], z_peer(d))
 
-    def gz_copy(d, c):
-        return remote(
-            lev.at[c, pl.ds(0, ROWS)], lev.at[c, pl.ds((Z - d) * ROWS, ROWS)],
-            gzs_sem.at[d - 1, c], gzr_sem.at[d - 1, c], z_peer(d),
-        )
-
-    def gx_copy(d, c):
-        return remote(
-            lev.at[c, pl.ds(0, zrows)], lev.at[c, pl.ds((X - d) * zrows, zrows)],
-            gxs_sem.at[d - 1, c], gxr_sem.at[d - 1, c], x_peer(d),
-        )
+    def place(t, part, c):
+        rows = pl.ds(pl.multiple_of(t * ROWS, ROWS), ROWS)
+        return lev.at[c, rows] if part == 0 else scales.at[rows]
+
+    def gather_copy(t, part, c, slot, peer):
+        ref = place(t, part, c)
+        at = c if part == 0 else nch
+        return remote(ref, ref, gs_sem.at[slot, at], gr_sem.at[slot, at], peer)
+
+    def right(k, part, c):
+        return gather_copy((z - k) * X + x, part, c, k, {"tensor": me + X})
+
+    def left(k, part, c):
+        return gather_copy((z + k) * X + x, part, c, Z + k, {"tensor": me - X})
+
+    def across(d, zz, part, c):
+        return gather_copy(zz * X + x, part, c, 2 * Z + (d - 1) * Z + zz, x_peer(d))
+
+    def each_part(c, act):
+        act(0)
+        pl.when(c == 0)(lambda: act(1))
+
+    def start_right(k, c):
+        @pl.when(jnp.logical_and(z - k >= 0, z < Z - 1))
+        def _():
+            each_part(c, lambda part: right(k, part, c).start())
+
+    def start_left(k, c):
+        @pl.when(jnp.logical_and(z + k < Z, z > 0))
+        def _():
+            each_part(c, lambda part: left(k, part, c).start())
+
+    def start_across(zz, c):
+        for d in range(1, X):
+            each_part(c, lambda part, d=d: across(d, zz, part, c).start())
 
     def loop(body):
         lax.fori_loop(0, nch, lambda c, _: (body(c), 0)[1], 0)
 
+    small = [
+        pltpu.make_async_copy(src, dst, small_sem.at[i])
+        for i, (src, dst) in enumerate((
+            (attn_h, attn), (wo_exp_h, wo_exp), (token_scale_h, token_scale), (residual_h, residual),
+            (gain_h, gain), (gate_exp_h, gate_exp), (up_exp_h, up_exp),
+        ))
+    ]
+    small[0].start()
     loop(lambda c: wo_copy(c).start())
+    for copy in small[1:]:
+        copy.start()
     gate_copy = pltpu.make_async_copy(gate, gate_v, weight_sem.at[0])
     up_copy = pltpu.make_async_copy(up, up_v, weight_sem.at[1])
     gate_copy.start()
@@ -93,6 +128,7 @@
     for d in range(1, Z):
         pl.semaphore_signal(barrier, inc=1, device_id=z_peer(d), device_id_type=MESH)
 
+    small[0].wait()
     for d in range(X):
         for dz in range(Z):
             a_rel[pl.ds((d * Z + dz) * ROWS, ROWS), :] = attn[
@@ -128,10 +164,12 @@
 
     loop(add_x)
 
-    row_of = lax.broadcasted_iota(jnp.int32, (ROWS, 1), 0)
-    row_scale = jnp.zeros((ROWS, 1), jnp.float32)
-    for i in range(ROWS):
-        row_scale = jnp.where(row_of == i, token_scale[i], row_scale)
+    for copy in small[1:]:
+        copy.wait()
+    square = (ROWS, ROWS)
+    diagonal = lax.broadcasted_iota(jnp.int32, square, 0) == lax.broadcasted_iota(jnp.int32, square, 1)
+    spread = jnp.where(diagonal, jnp.broadcast_to(token_scale[...], square), 0.0)
+    row_scale = jnp.sum(spread, axis=1, keepdims=True)
 
     def add_z(c, squares):
         for d in range(1, Z):
@@ -158,11 +196,14 @@
     xscale = ((largest + 1e-06) / 127.0).astype(jnp.bfloat16)
     xwide = xscale.astype(jnp.float32)
 
+    own_rows = pl.ds(pl.multiple_of(me * ROWS, ROWS), ROWS)
+    scales[own_rows, :] = jnp.broadcast_to(xwide, (ROWS, EXTRA)).astype(jnp.bfloat16)
+
     def send(c):
-        lev[c, :ROWS, :cw] = jnp.floor(total[c] / xwide + 0.5).astype(jnp.bfloat16)
-        lev[c, :ROWS, cw:] = jnp.broadcast_to(xwide, (ROWS, EXTRA)).astype(jnp.bfloat16)
-        for d in range(1, Z):
-            gz_copy(d, c).start()
+        lev[c, own_rows, :] = jnp.floor(total[c] / xwide + 0.5).astype(jnp.bfloat16)
+        start_right(0, c)
+        start_left(0, c)
+        start_across(z, c)
 
     loop(send)
     gate_acc[...] = jnp.zeros_like(gate_acc)
@@ -170,47 +211,67 @@
     gate_copy.wait()
     up_copy.wait()
 
-    def forward(c):
-        for d in range(1, Z):
-            gz_copy(d, c).wait_recv()
-        for d in range(1, X):
-            gx_copy(d, c).start()
+    def relay(k, c):
+        @pl.when(z - 1 - k >= 0)
+        def _():
+            each_part(c, lambda part: right(k, part, c).wait_recv())
+            start_right(k + 1, c)
+            start_across(z - 1 - k, c)
+
+        @pl.when(z + 1 + k < Z)
+        def _():
+            each_part(c, lambda part: left(k, part, c).wait_recv())
+            start_left(k + 1, c)
+            start_across(z + 1 + k, c)
 
     def multiply(c):
         for d in range(1, X):
-            gx_copy(d, c).wait_recv()
-        levels = lev[c, :, :cw]
+            for zz in range(Z):
+                each_part(c, lambda part, d=d, zz=zz: across(d, zz, part, c).wait_recv())
+        levels = lev[c]
         gate_acc[...] += jnp.dot(levels, gate_v[cols(c), :], preferred_element_type=jnp.float32)
         up_acc[...] += jnp.dot(levels, up_v[cols(c), :], preferred_element_type=jnp.float32)
 
-    forward(0)
-
-    def gather(c, _):
-        forward(c + 1)
-        multiply(c)
+    def gather(step, _):
+        for k in range(Z - 1):
+            c = step - k
+
+            @pl.when(jnp.logical_and(c >= 0, c < nch))
+            def _(k=k, c=c):
+                relay(k, c)
+
+        @pl.when(step >= Z)
+        def _():
+            multiply(step - Z)
+
         return 0
 
-    lax.fori_loop(0, nch - 1, gather, 0)
-    multiply(nch - 1)
+    lax.fori_loop(0, nch + Z, gather, 0)
 
     gate_scale = jnp.exp2(gate_exp[...].astype(jnp.float32))
     up_scale = jnp.exp2(up_exp[...].astype(jnp.float32))
-    for d in range(X):
-        for dz in range(Z):
-            rows = pl.ds((d * Z + dz) * ROWS, ROWS)
-            scale = lev[0, rows, cw:].astype(jnp.float32)[:, :1]
-            g = gate_acc[rows, :] * scale * gate_scale
-            u = up_acc[rows, :] * scale * up_scale
-            value = g / (1.0 + jnp.exp(-g)) * u
-            hidden[pl.ds(pl.multiple_of(block_of(d, dz) * ROWS, ROWS), ROWS), :] = value.astype(jnp.bfloat16)
+    for t in range(X * Z):
+        rows = pl.ds(t * ROWS, ROWS)
+        scale = scales[rows, :].astype(jnp.float32)[:, :1]
+        g = gate_acc[rows, :] * scale * gate_scale
+        u = up_acc[rows, :] * scale * up_scale
+        hidden[rows, :] = (g / (1.0 + jnp.exp(-g)) * u).astype(jnp.bfloat16)
 
     def drain(c):
         for d in range(1, X):
             x_copy(d, c).wait_send()
-            gx_copy(d, c).wait_send()
+            for zz in range(Z):
+                each_part(c, lambda part, d=d, zz=zz: across(d, zz, part, c).wait_send())
         for d in range(1, Z):
             z_copy(d, c).wait_send()
-            gz_copy(d, c).wait_send()
+        for k in range(Z):
+            @pl.when(jnp.logical_and(z - k >= 0, z < Z - 1))
+            def _(k=k):
+                each_part(c, lambda part: right(k, part, c).wait_send())
+
+            @pl.when(jnp.logical_and(z + k < Z, z > 0))
+            def _(k=k):
+                each_part(c, lambda part: left(k, part, c).wait_send())
 
     loop(drain)
 
@@ -232,11 +293,16 @@
             jax.ShapeDtypeStruct((rows, ff), jnp.bfloat16),
             jax.ShapeDtypeStruct((1, D), jnp.float32),
         ),
-        in_specs=[
-            vmem, anywhere, vmem, pl.BlockSpec(memory_space=pltpu.SMEM), vmem, vmem, anywhere, anywhere, vmem, vmem,
-        ],
+        in_specs=[anywhere] * 10,
         out_specs=(vmem, vmem),
         scratch_shapes=[
+            pltpu.VMEM(attn_in.shape, jnp.bfloat16),
+            pltpu.VMEM((1, D), jnp.int32),
+            pltpu.VMEM((1, ROWS), jnp.float32),
+            pltpu.VMEM(residual.shape, jnp.bfloat16),
+            pltpu.VMEM((1, D), jnp.float32),
+            pltpu.VMEM((1, ff), jnp.int32),
+            pltpu.VMEM((1, ff), jnp.int32),
             pltpu.VMEM(wo_int.shape, jnp.bfloat16),
             pltpu.VMEM(gate_int.shape, jnp.bfloat16),
             pltpu.VMEM(up_int.shape, jnp.bfloat16),
@@ -248,29 +314,29 @@
             pltpu.VMEM((zn, nch, ROWS, cw + EXTRA), jnp.int16),
             pltpu.VMEM((zn, nch, ROWS, cw + EXTRA), jnp.int16),
             pltpu.VMEM((nch, ROWS, cw), jnp.float32),
-            pltpu.VMEM((nch, rows, cw + EXTRA), jnp.bfloat16),
+            pltpu.VMEM((nch, rows, cw), jnp.bfloat16),
+            pltpu.VMEM((rows, EXTRA), jnp.bfloat16),
             pltpu.VMEM((rows, ff), jnp.float32),
             pltpu.VMEM((rows, ff), jnp.float32),
+            dma((7,)),
             dma((nch,)),
             dma((2,)),
             dma((xn, nch)),
             dma((xn, nch)),
             dma((zn, nch)),
             dma((zn, nch)),
-            dma((zn, nch)),
-            dma((zn, nch)),
-            dma((xn, nch)),
-            dma((xn, nch)),
+            dma((2 * Z + xn * Z, nch + 1)),
+            dma((2 * Z + xn * Z, nch + 1)),
         ],
         compiler_params=pltpu.CompilerParams(
-            collective_id=0, has_side_effects=True, vmem_limit_bytes=48 * 1024 * 1024
+            collective_id=0, has_side_effects=True, vmem_limit_bytes=60 * 1024 * 1024
         ),
         cost_estimate=pl.CostEstimate(
             flops=2 * rows * D * (attn_in.shape[1] + 2 * ff), bytes_accessed=2 * D * (attn_in.shape[1] + 2 * ff),
             transcendentals=rows * ff,
         ),
     )(
-        attn_in, wo_int, wo_exponent.reshape(1, D), token_scale, residual, norm_gain.reshape(1, D),
+        attn_in, wo_int, wo_exponent.reshape(1, D), token_scale.reshape(1, ROWS), residual, norm_gain.reshape(1, D),
         gate_int, up_int, gate_exponent.reshape(1, ff), up_exponent.reshape(1, ff),
     )
 

time: 85.2 us -> 72 us (0.85)
  Pallas kernels: 75.4 us -> 68.2 us
  local copies, waits for them, and re-layouts: 8.74 us -> 2.85 us
    pallas_call x1, Pallas kernels: 75.4 us -> 68.2 us  [local(): pl.pallas_call(functools.partial(kernel, X, Z, nch), out_shape=(jax.Shape...]
    unnamed x18 -> x2, local copies, waits for them, and re-layouts: 8.74 us -> 2.85 us
where the time goes in v2:
time: 72 us; the launch traced here: 71.7 us
  Pallas kernels  68.2 us (95%)
  local copies, waits for them, and re-layouts  2.85 us (4%)
    pallas_call x1, Pallas kernels, local(): pl.pallas_call(functools.partial(kernel, X, Z, nch), out_shape=(jax.Shape...  68.2 us
    unnamed x2, local copies, waits for them, and re-layouts  2.85 us

profile of v2, /device:TPU:0, one launch (start us, length us, event | category | flops | bytes accessed | tf_op | source)
XLA Modules:
  0.0 71.7 jit_solution(15936132886791840451)
XLA Ops:
  0.6 68.2 %shard_map.113 = (bf16[128,256]{1,0:T(8,128)(2,1)}, f32[1,8192]{1,0:T(1,128)}) custom-call(bf16[128,256]{1,0:T(8,128)(2,1)} %attn_h.1, bf16[256,8192]{1,0:T(8,128)(2,1)} %wo.1, s32[1,8192]{1,0:T(1,128)} %bitcast.5, f32[1,16]{1,0:T(1,128)} %bitcast.9, bf16[16,8192]{1,0:T(8,128)(2,1)} %residual_h.1, f32[1,8192]{1,0:T(1,128)} %bitcast.6, ...), custom_call_target="tpu_custom_call" | custom-call | flops 1610612736 | bytes 12582912 | tf_op jit(solution)/shard_map/pallas_call | solution.py:290
  68.9 1.5 %copy.14 = bf16[128,256]{1,0:T(8,128)(2,1)} copy(bf16[128,256]{1,0:T(8,128)(2,1)} %get-tuple-element.4) | data formatting | bytes 131072
  70.4 1.4 %copy.15 = f32[1,8192]{1,0:T(1,128)} copy(f32[1,8192]{1,0:T(1,128)} %get-tuple-element.5) | data formatting | bytes 65536
